TPU v7x, 1024 devices: a whole 4x4x32 slice. The times are simulated.
1024 devices in a mesh: replica: 16 (over x, z_hi), fsdp: 8 (over z_lo), tensor: 8 (over y, core).
Axes of the slice: x: 4, y: 4, z: 32 (z_hi: 4, z_lo: 8; z = z_hi * 8 + z_lo), core: 2. Of those that a mesh axis runs over, the one named last changes fastest.
Arguments:
- master: float32 [8192, 8, 2048], P(('fsdp', 'tensor'), None, 'replica'), may hold values from -6 to 6
- gradient: bfloat16 [8192, 8, 2048], P(('fsdp', 'tensor'), None, 'replica'), may hold values from -6 to 6
- first_moment: float32 [8192, 8, 2048], P(('fsdp', 'tensor'), None, 'replica'), may hold values from -3 to 3
- second_moment: float32 [8192, 8, 2048], P(('fsdp', 'tensor'), None, 'replica'), may hold values from 0.1 to 4
Outputs:
- new_master: float32 [8192, 8, 2048], P(('fsdp', 'tensor'), None, 'replica')
- rollout: bfloat16 [8192, 8, 2048], P('fsdp', 'tensor')
All inputs are finite; a program needn't handle non-finite values.
Results may differ from a plain program's by a relative error of at most 0.001.
Values may be sent and summed in bfloat16 or wider, within the bound.
No kernel may reach another device: no remote copies, remote signals or barrier semaphores. Data moves between devices by JAX's collectives and lax.ppermute only.
A program may use at most 32 MiB of HBM per device.

v0:
```python
import jax
import jax.numpy as jnp
from jax import lax
from jax.sharding import PartitionSpec as P


def adamw_update(master, gradient, first_moment, second_moment):
    grad_full = gradient.astype(jnp.float32)
    moment_one = 0.9 * first_moment + 0.1 * grad_full
    moment_two = 0.95 * second_moment + 0.05 * grad_full * grad_full
    corr_one = 1.0 - 0.9**10
    corr_two = 1.0 - 0.95**10
    step_size = moment_one / corr_one / (jnp.sqrt(moment_two / corr_two) + 1e-08)
    return master * (1.0 - 0.1 * 0.1) - 0.1 * step_size


def on_device(master, gradient, first_moment, second_moment):
    new_master = adamw_update(master, gradient, first_moment, second_moment)
    sliced = lax.all_to_all(
        new_master.astype(jnp.bfloat16), "tensor", split_axis=1, concat_axis=0, tiled=True
    )
    rollout = lax.all_gather(sliced, "replica", axis=2, tiled=True)
    return (new_master, rollout)


def solution(mesh):
    placed = (
        P(("fsdp", "tensor"), None, "replica"),
        P(("fsdp", "tensor"), None, "replica"),
        P(("fsdp", "tensor"), None, "replica"),
        P(("fsdp", "tensor"), None, "replica"),
    )
    return jax.shard_map(
        on_device,
        mesh=mesh,
        in_specs=placed,
        out_specs=(P(("fsdp", "tensor"), None, "replica"), P("fsdp", "tensor", None)),
        check_vma=False,
    )
```

profile of v0, /device:TPU:14, one launch (start us, length us, event | category | flops | bytes accessed | tf_op | source)
XLA Modules:
  0.0 307.1 jit_solution(4416268146281402251)
XLA Ops:
  7.2 0.0 all-gather.2.cloned.1.call-start
  7.2 2.0 fusion.9
  9.2 10.9 %all_to_all.18 = bf16[128,8,128]{2,0,1:T(8,128)(2,1)} all-to-all(bf16[128,8,128]{2,0,1:T(8,128)(2,1)S(1)} %get-tuple-element.4), channel_id=1, replica_groups=mesh['replica'=16,'fsdp'=8,'tensor'=8] {'tensor'}, dimensions={1} | all-to-all | bytes 524288 | tf_op jit(solution)/shard_map/all_to_all | solution.py:19
  20.1 0.0 all-gather.2.cloned.1.call-update
  20.1 1.1 copy.11
  21.2 274.3 %all-gather.2.cloned.1.call-done = bf16[1024,1,2048]{2,0,1:T(8,128)(2,1)} async-done(((bf16[1024,1,128]{2,0,1:T(8,128)(2,1)}), bf16[1024,1,2048]{2,0,1:T(8,128)(2,1)}) %all-gather.2.cloned.1.call-update) | async-done | bytes 4194320 | tf_op jit(solution)/shard_map/all_gather | solution.py:22
  295.5 4.8 %copy.27 = bf16[1024,1,2048]{2,0,1:T(8,128)(2,1)} copy(bf16[1024,1,2048]{2,0,1:T(8,128)(2,1)} %all-gather.2.cloned.1.call-done) | data formatting | bytes 8388608
Async XLA Ops:
  7.2 288.3 %all-gather.2.cloned.1.call-start = ((), (), s32[]{:S(2)}) async-start(), calls=%async_computation.1 | async-start | bytes 4456448 | tf_op jit(solution)/shard_map/all_gather | solution.py:22
Sparse Core Ops, SparseCore 0:
  20.2 275.2 all-gather.1
where the time goes:
time: 307 us
  waiting for transfers between devices  274 us (89%)
  between operations  14 us (5%)
  blocking collectives  10.9 us (4%)
  local copies, waits for them, and re-layouts  5.89 us (2%)
    all_gather x1, waiting for transfers between devices, on_device(): rollout = lax.all_gather(sliced, 'replica', axis=2, tiled=True)  274 us
    all_to_all x1, blocking collectives, on_device(): lax.all_to_all(new_master.astype(jnp.bfloat16), 'tensor', split_axis=1, c...  10.9 us
  transfers between devices with their start and end apart: 1, of which 1 were waited for; matrix products, arithmetic and copies ran while one was open for 0% of the time, Pallas kernels for 0%

commit v1 on v0

v1 whole, which is shorter than its diff:
```python
import functools
import jax
import jax.numpy as jnp
from jax import lax
from jax.sharding import Mesh, PartitionSpec as P
from jax.experimental import pallas as pl
from jax.experimental.pallas import tpu as pltpu

NX, NH, LANES = 4, 4, 128


def adamw_update(master, gradient, first_moment, second_moment):
    grad_full = gradient.astype(jnp.float32)
    moment_one = 0.9 * first_moment + 0.1 * grad_full
    moment_two = 0.95 * second_moment + 0.05 * grad_full * grad_full
    corr_one = 1.0 - 0.9**10
    corr_two = 1.0 - 0.95**10
    step_size = moment_one / corr_one / (jnp.sqrt(moment_two / corr_two) + 1e-08)
    return master * (1.0 - 0.1 * 0.1) - 0.1 * step_size


def ring(axis, block, step):
    n = lax.axis_size(axis)
    return lax.ppermute(block, axis, [(i, (i + step) % n) for i in range(n)])


def onward(axis, fore, back):
    n, m = lax.axis_size(axis), lax.axis_size("tensor")
    pairs = [
        (i * m + t, (i + (1 if t % 2 == 0 else -1)) % n * m + t)
        for i in range(n)
        for t in range(m)
    ]
    core = lax.axis_index("tensor") % 2
    return lax.ppermute(jnp.where(core == 0, fore, back), (axis, "tensor"), pairs)


def around(axis, block):
    fore, back = ring(axis, block, 1), ring(axis, block, -1)
    fore, back = lax.optimization_barrier((fore, back))
    return [block, fore, back, onward(axis, fore, back)]


STEPS = (0, 1, -1, 2)


def place_kernel(parts, *refs):
    out = refs[-1]
    h = lax.axis_index("h")
    for ref, places in zip(refs[:-1], parts):
        for k, (dx, dh) in enumerate(places):
            col = lax.rem(h - dh + NH, NH) + NH * dx
            out[:, pl.ds(pl.multiple_of(col * LANES, LANES), LANES)] = ref[k]


def place(blocks, parts, rows, tile=256):
    return pl.pallas_call(
        functools.partial(place_kernel, parts),
        grid=(rows // tile,),
        out_shape=jax.ShapeDtypeStruct((rows, NX * NH * LANES), jnp.bfloat16),
        in_specs=[
            pl.BlockSpec((len(p), tile, LANES), lambda i: (0, i, 0)) for p in parts
        ],
        out_specs=pl.BlockSpec((tile, NX * NH * LANES), lambda i: (i, 0)),
        cost_estimate=pl.CostEstimate(
            flops=0, bytes_accessed=rows * NX * NH * LANES * 4, transcendentals=0
        ),
    )(*blocks)


def on_device(master, gradient, first_moment, second_moment):
    new_master = adamw_update(master, gradient, first_moment, second_moment)
    own = lax.all_to_all(
        new_master.astype(jnp.bfloat16), "tensor", split_axis=1, concat_axis=0, tiled=True
    )
    rows = own.shape[0]
    own = own.reshape(1, rows, LANES)
    own, up, down, far = around("h", own)
    blocks, parts = [], []
    for block, steps in (
        (own, (0,)),
        (jnp.concatenate([up, down]), (1, -1)),
        (far, (2,)),
    ):
        if blocks:
            block, blocks[-1] = lax.optimization_barrier((block, blocks[-1]))
        blocks.append(lax.all_gather(block, "x", axis=0, tiled=True))
        parts.append([(x, dh) for x in range(NX) for dh in steps])
    return (new_master, place(blocks, parts, rows)[:, None, :])


def solution(mesh):
    grid = mesh.devices
    fine = Mesh(
        grid.reshape(NX, NH, *grid.shape[1:]), ("x", "h", *mesh.axis_names[1:])
    )
    placed = P(("fsdp", "tensor"), None, ("x", "h"))
    return jax.shard_map(
        on_device,
        mesh=fine,
        in_specs=(placed,) * 4,
        out_specs=(placed, P("fsdp", "tensor", None)),
        check_vma=False,
    )
```

time: 307 us -> 194 us (0.63)
  the two profiles are of different devices: /device:TPU:14 before, /device:TPU:1 now
where the time goes in v1:
time: 194 us
  waiting for transfers between devices  122 us (63%)
  starting transfers between devices  25.2 us (13%)
  blocking collectives  23.7 us (12%)
  between operations  13.8 us (7%)
  Pallas kernels  5.08 us (3%)
  other arithmetic  2.83 us (1%)
    all_gather x3, waiting for transfers between devices, on_device(): blocks.append(lax.all_gather(block, 'x', axis=0, tiled=True))  77.4 us
    ppermute x2, waiting for transfers between devices, ring(): return lax.ppermute(block, axis, [(i, (i + step) % n) for i in range(n)])  37.9 us
    all_to_all x1, blocking collectives, on_device(): lax.all_to_all(new_master.astype(jnp.bfloat16), 'tensor', split_axis=1, c...  23.7 us
    ppermute x2, starting transfers between devices, ring(): return lax.ppermute(block, axis, [(i, (i + step) % n) for i in range(n)])  14 us
    ppermute x1, starting transfers between devices, onward(): lax.ppermute(jnp.where(core == 0, fore, back), (axis, 'tensor'), pairs)  11.1 us
    ppermute x1, waiting for transfers between devices, onward(): lax.ppermute(jnp.where(core == 0, fore, back), (axis, 'tensor'), pairs)  6.35 us
    pallas_call x1, Pallas kernels, place(): pl.pallas_call(functools.partial(place_kernel, parts), grid=(rows // tile...  5.08 us
  transfers between devices with their start and end apart: 6, of which 4 were waited for; matrix products, arithmetic and copies ran while one was open for 1% of the time, Pallas kernels for 0%

profile of v1, /device:TPU:1, one launch (start us, length us, event | category | flops | bytes accessed | tf_op | source)
XLA Modules:
  0.0 193.5 jit_solution(15556171085681127300)
XLA Ops:
  7.2 0.0 all-gather.4.cloned.1.call-start
  7.2 2.0 %fusion.9 = (bf16[128,8,128]{2,0,1:T(8,128)(2,1)S(1)}, f32[128,8,128]{2,0,1:T(8,128)S(1)}) fusion(f32[128,8,128]{2,1,0:T(8,128)} %param.7, bf16[128,8,128]{2,1,0:T(8,128)(2,1)} %param.5, f32[128,8,128]{2,1,0:T(8,128)} %param.6, f32[128,8,128]{2,1,0:T(8,128)} %param.4), kind=kLoop, calls=%fused_computation.16 | loop fusion | flops 2097152 | bytes 2621440 | tf_op jit(solution)/shard_map/convert_element_type | solution.py:74
  9.2 23.7 %all_to_all.15 = bf16[128,8,128]{2,0,1:T(8,128)(2,1)} all-to-all(bf16[128,8,128]{2,0,1:T(8,128)(2,1)S(1)} %get-tuple-element.16), channel_id=1, replica_groups=mesh['x'=4,'h'=4,'fsdp'=8,'tensor'=8] {'tensor'}, dimensions={1} | all-to-all | bytes 524288 | tf_op jit(solution)/shard_map/all_to_all | solution.py:73
  32.9 0.0 all-gather.4.cloned.1.call-update
  32.9 0.0 all-gather.6.cloned.1.call-start
  33.0 11.4 %collective-permute-start.1 = (bf16[1,1024,128]{2,1,0:T(8,128)(2,1)}, bf16[1,1024,128]{2,1,0:T(8,128)(2,1)S(1)}, u32[]{:S(2)}, u32[]{:S(2)}) collective-permute-start(bf16[1,1024,128]{2,1,0:T(8,128)(2,1)} %bitcast.8), channel_id=1, source_target_pairs={{0,192},{64,0},{128,64},{192,128},{1,193},{65,1},{129,65},{193,129... | collective-permute-start | bytes 786440 | tf_op jit(solution)/shard_map/ppermute | solution.py:24
  44.3 2.6 %collective-permute-start = (bf16[1,1024,128]{2,1,0:T(8,128)(2,1)}, bf16[1,1024,128]{2,1,0:T(8,128)(2,1)S(1)}, u32[]{:S(2)}, u32[]{:S(2)}) collective-permute-start(bf16[1,1024,128]{2,1,0:T(8,128)(2,1)} %bitcast.9), channel_id=1, source_target_pairs={{0,64},{64,128},{128,192},{192,0},{1,65},{65,129},{129,193},{193,1... | collective-permute-start | bytes 786440 | tf_op jit(solution)/shard_map/ppermute | solution.py:24
  47.0 37.9 %collective-permute-done.1 = bf16[1,1024,128]{2,1,0:T(8,128)(2,1)S(1)} collective-permute-done((bf16[1,1024,128]{2,1,0:T(8,128)(2,1)}, bf16[1,1024,128]{2,1,0:T(8,128)(2,1)S(1)}, u32[]{:S(2)}, u32[]{:S(2)}) %collective-permute-start.1) | collective-permute-done | bytes 262176 | tf_op jit(solution)/shard_map/ppermute | solution.py:24
  84.9 0.0 collective-permute-done
  84.9 0.8 pad_maximum_fusion
  85.7 0.0 all-gather.4.cloned.1.call-done.refs_0_
  85.7 0.0 all-gather.6.cloned.1.call-update
  85.8 0.0 all-gather.8.cloned.1.call-start
  85.9 11.1 %collective-permute-start.2 = (bf16[1,1024,128]{2,1,0:T(8,128)(2,1)S(1)}, bf16[1,1024,128]{2,1,0:T(8,128)(2,1)S(1)}, u32[]{:S(2)}, u32[]{:S(2)}) collective-permute-start(bf16[1,1024,128]{2,1,0:T(8,128)(2,1)S(1)} %broadcast_select_fusion), channel_id=1, source_target_pairs={{0,64},{1,193},{2,66},{3,195},{4,68},{5,197},{6,70},{7,199},{64,12... | collective-permute-start | bytes 786440 | tf_op jit(solution)/shard_map/ppermute | solution.py:35
  97.0 6.3 %collective-permute-done.2 = bf16[1,1024,128]{2,1,0:T(8,128)(2,1)S(1)} collective-permute-done((bf16[1,1024,128]{2,1,0:T(8,128)(2,1)S(1)}, bf16[1,1024,128]{2,1,0:T(8,128)(2,1)S(1)}, u32[]{:S(2)}, u32[]{:S(2)}) %collective-permute-start.2) | collective-permute-done | bytes 262176 | tf_op jit(solution)/shard_map/ppermute | solution.py:35
  103.3 0.0 copy-start
  103.3 34.1 %all-gather.6.cloned.1.call-done.refs_1_ = bf16[8,1024,128]{2,1,0:T(8,128)(2,1)} async-done(((bf16[2,1024,128]{2,1,0:T(8,128)(2,1)}), bf16[8,1024,128]{2,1,0:T(8,128)(2,1)}) %all-gather.6.cloned.1.call-update) | async-done | bytes 2097168 | tf_op jit(solution)/shard_map/all_gather | solution.py:87
  137.4 0.0 copy-done
  137.4 0.0 all-gather.8.cloned.1.call-update
  137.5 1.1 copy.11
  138.6 43.3 %all-gather.8.cloned.1.call-done.refs_2_ = bf16[4,1024,128]{2,1,0:T(8,128)(2,1)} async-done(((bf16[1,1024,128]{2,1,0:T(8,128)(2,1)}), bf16[4,1024,128]{2,1,0:T(8,128)(2,1)}) %all-gather.8.cloned.1.call-update) | async-done | bytes 1048592 | tf_op jit(solution)/shard_map/all_gather | solution.py:87
  181.9 5.1 %shard_map.59 = bf16[1024,2048]{1,0:T(8,128)(2,1)} custom-call(bf16[4,1024,128]{2,1,0:T(8,128)(2,1)} %all-gather.4.cloned.1.call-done.refs_0_, bf16[8,1024,128]{2,1,0:T(8,128)(2,1)} %all-gather.6.cloned.1.call-done.refs_1_, bf16[4,1024,128]{2,1,0:T(8,128)(2,1)} %all-gather.8.cloned.1.call-done.refs_2_), custom_call_target="tpu_custom_call" | custom-call | bytes 8388608 | tf_op jit(solution)/shard_map/pallas_call | solution.py:57
  (1 shorter events, 0.0 us)
Async XLA Ops:
  7.2 78.6 %all-gather.4.cloned.1.call-start = ((), (), s32[]{:S(2)}) async-start(), calls=%async_computation.1 | async-start | bytes 1310720 | tf_op jit(solution)/shard_map/all_gather | solution.py:87
  32.9 104.5 %all-gather.6.cloned.1.call-start = ((), (), s32[]{:S(2)}) async-start(), calls=%async_computation.2 | async-start | bytes 2621440 | tf_op jit(solution)/shard_map/all_gather | solution.py:87
  33.0 51.9 %collective-permute-start.1 = (bf16[1,1024,128]{2,1,0:T(8,128)(2,1)}, bf16[1,1024,128]{2,1,0:T(8,128)(2,1)S(1)}, u32[]{:S(2)}, u32[]{:S(2)}) collective-permute-start(bf16[1,1024,128]{2,1,0:T(8,128)(2,1)} %bitcast.8), channel_id=1, source_target_pairs={{0,192},{64,0},{128,64},{192,128},{1,193},{65,1},{129,65},{193,129... | collective-permute-start | bytes 786440 | tf_op jit(solution)/shard_map/ppermute | solution.py:24
  44.3 40.5 %collective-permute-start = (bf16[1,1024,128]{2,1,0:T(8,128)(2,1)}, bf16[1,1024,128]{2,1,0:T(8,128)(2,1)S(1)}, u32[]{:S(2)}, u32[]{:S(2)}) collective-permute-start(bf16[1,1024,128]{2,1,0:T(8,128)(2,1)} %bitcast.9), channel_id=1, source_target_pairs={{0,64},{64,128},{128,192},{192,0},{1,65},{65,129},{129,193},{193,1... | collective-permute-start | bytes 786440 | tf_op jit(solution)/shard_map/ppermute | solution.py:24
  85.8 96.1 %all-gather.8.cloned.1.call-start = ((), (), s32[]{:S(2)}) async-start(), calls=%async_computation.3 | async-start | bytes 1310720 | tf_op jit(solution)/shard_map/all_gather | solution.py:87
  85.9 17.5 %collective-permute-start.2 = (bf16[1,1024,128]{2,1,0:T(8,128)(2,1)S(1)}, bf16[1,1024,128]{2,1,0:T(8,128)(2,1)S(1)}, u32[]{:S(2)}, u32[]{:S(2)}) collective-permute-start(bf16[1,1024,128]{2,1,0:T(8,128)(2,1)S(1)} %broadcast_select_fusion), channel_id=1, source_target_pairs={{0,64},{1,193},{2,66},{3,195},{4,68},{5,197},{6,70},{7,199},{64,12... | collective-permute-start | bytes 786440 | tf_op jit(solution)/shard_map/ppermute | solution.py:35
  103.3 34.1 %copy-start = (bf16[1,1024,128]{2,1,0:T(8,128)(2,1)}, bf16[1,1024,128]{2,1,0:T(8,128)(2,1)S(1)}, u32[]{:S(2)}) copy-start(bf16[1,1024,128]{2,1,0:T(8,128)(2,1)S(1)} %collective-permute-done.2) | copy-start | bytes 786436
Sparse Core Ops, SparseCore 0:
  33.0 35.4 all-gather.3
  85.9 51.5 all-gather.5
  140.7 41.1 all-gather.7

commit v2 on v1

--- a/solution.py
+++ b/solution.py
@@ -35,15 +35,6 @@
     return lax.ppermute(jnp.where(core == 0, fore, back), (axis, "tensor"), pairs)
 
 
-def around(axis, block):
-    fore, back = ring(axis, block, 1), ring(axis, block, -1)
-    fore, back = lax.optimization_barrier((fore, back))
-    return [block, fore, back, onward(axis, fore, back)]
-
-
-STEPS = (0, 1, -1, 2)
-
-
 def place_kernel(parts, *refs):
     out = refs[-1]
     h = lax.axis_index("h")
@@ -68,6 +59,43 @@
     )(*blocks)
 
 
+def insert_kernel(col, block, base, out):
+    del col, base
+    out[...] = block[0]
+
+
+def insert(rollout, block, dh):
+    rows = block.shape[1]
+    col = lax.rem(lax.axis_index("h") - dh + NH, NH).astype(jnp.int32)
+    return pl.pallas_call(
+        insert_kernel,
+        grid_spec=pltpu.PrefetchScalarGridSpec(
+            num_scalar_prefetch=1,
+            grid=(NX, SPLIT),
+            in_specs=[
+                pl.BlockSpec((1, rows // SPLIT, LANES), lambda x, i, col: (x, i, 0)),
+                pl.BlockSpec(memory_space=pl.ANY),
+            ],
+            out_specs=pl.BlockSpec(
+                (rows // SPLIT, LANES), lambda x, i, col: (i, x * NH + col[0])
+            ),
+        ),
+        out_shape=jax.ShapeDtypeStruct(rollout.shape, rollout.dtype),
+        input_output_aliases={2: 0},
+        cost_estimate=pl.CostEstimate(
+            flops=0, bytes_accessed=4 * block.size, transcendentals=0
+        ),
+    )(col[None], block, rollout)
+
+
+SPLIT = 1
+
+
+def exchange(block):
+    copies = jnp.broadcast_to(block[None], (NX, *block.shape))
+    return lax.all_to_all(copies, "x", 0, 0).reshape(-1, *block.shape[1:])
+
+
 def on_device(master, gradient, first_moment, second_moment):
     new_master = adamw_update(master, gradient, first_moment, second_moment)
     own = lax.all_to_all(
@@ -75,18 +103,23 @@
     )
     rows = own.shape[0]
     own = own.reshape(1, rows, LANES)
-    own, up, down, far = around("h", own)
-    blocks, parts = [], []
-    for block, steps in (
-        (own, (0,)),
-        (jnp.concatenate([up, down]), (1, -1)),
-        (far, (2,)),
-    ):
-        if blocks:
-            block, blocks[-1] = lax.optimization_barrier((block, blocks[-1]))
-        blocks.append(lax.all_gather(block, "x", axis=0, tiled=True))
-        parts.append([(x, dh) for x in range(NX) for dh in steps])
-    return (new_master, place(blocks, parts, rows)[:, None, :])
+    halves = [
+        lax.all_gather(part, "x", axis=0, tiled=True)
+        for part in jnp.split(own, 2, axis=1)
+    ]
+    up, down = ring("h", own, 1), ring("h", own, -1)
+    up, down, halves = lax.optimization_barrier((up, down, halves))
+    far = onward("h", up, down)
+    near = exchange(jnp.concatenate([up, down]))
+    own = jnp.concatenate(halves, axis=1)
+    parts = [
+        [(x, 0) for x in range(NX)],
+        [(x, dh) for x in range(NX) for dh in (1, -1)],
+    ]
+    rollout = place([own, near], parts, rows)
+    far, near = lax.optimization_barrier((far, near))
+    rollout = insert(rollout, exchange(far), 2)
+    return (new_master, rollout[:, None, :])
 
 
 def solution(mesh):

time: 194 us -> 146 us (0.75); the launches traced: 194 us -> 143 us
  waiting for transfers between devices: 122 us -> 36.8 us
  blocking collectives: 23.7 us -> 46.4 us
  starting transfers between devices: 25.2 us -> 39.6 us
  between operations: 13.8 us -> 0.7 us
  local copies, waits for them, and re-layouts: 1.1 us -> 5.99 us
  Pallas kernels: 5.08 us -> 8.07 us
  other arithmetic: 2.83 us -> 5.11 us
    all_gather x3 -> x0, waiting for transfers between devices: 77.4 us -> none  [on_device(): blocks.append(lax.all_gather(block, 'x', axis=0, tiled=True))]
    all_gather x0 -> x2, blocking collectives: none -> 23.4 us  [on_device(): lax.all_gather(part, 'x', axis=0, tiled=True)]
    ppermute x2, waiting for transfers between devices: 37.9 us -> 15 us  [ring(): return lax.ppermute(block, axis, [(i, (i + step) % n) for i in range(n)])]
    ppermute x1, waiting for transfers between devices: 6.35 us -> 21.2 us  [onward(): lax.ppermute(jnp.where(core == 0, fore, back), (axis, 'tensor'), pairs)]
    all_to_all x0 -> x2, starting transfers between devices: none -> 7.81 us  [exchange(): return lax.all_to_all(copies, 'x', 0, 0).reshape(-1, *block.shape[1:])]
    ppermute x1, starting transfers between devices: 11.1 us -> 17.8 us  [onward(): lax.ppermute(jnp.where(core == 0, fore, back), (axis, 'tensor'), pairs)]
    pallas_call x0 -> x1, Pallas kernels: none -> 3.36 us  [insert(): pl.pallas_call(insert_kernel, grid_spec=pltpu.PrefetchScalarGridSpec(num_...]
    broadcast_in_dim x0 -> x2, local copies, waits for them, and re-layouts: none -> 2.85 us  [exchange(): copies = jnp.broadcast_to(block[None], (NX, *block.shape))]
  transfers between devices with their start and end apart: 6 -> 5, of which waited for: 4 -> 3; matrix products, arithmetic and copies ran while one was open for 1% -> 3% of each run, Pallas kernels for 0% -> 3%
where the time goes in v2:
time: 146 us; the launch traced here: 143 us
  blocking collectives  46.4 us (32%)
  starting transfers between devices  39.6 us (27%)
  waiting for transfers between devices  36.8 us (25%)
  Pallas kernels  8.07 us (6%)
  local copies, waits for them, and re-layouts  5.99 us (4%)
  other arithmetic  5.11 us (4%)
    all_gather x2, blocking collectives, on_device(): lax.all_gather(part, 'x', axis=0, tiled=True)  23.4 us
    all_to_all x1, blocking collectives, on_device(): lax.all_to_all(new_master.astype(jnp.bfloat16), 'tensor', split_axis=1, c...  23 us
    ppermute x1, waiting for transfers between devices, onward(): lax.ppermute(jnp.where(core == 0, fore, back), (axis, 'tensor'), pairs)  21.2 us
    ppermute x1, starting transfers between devices, onward(): lax.ppermute(jnp.where(core == 0, fore, back), (axis, 'tensor'), pairs)  17.8 us
    ppermute x2, waiting for transfers between devices, ring(): return lax.ppermute(block, axis, [(i, (i + step) % n) for i in range(n)])  15 us
    ppermute x2, starting transfers between devices, ring(): return lax.ppermute(block, axis, [(i, (i + step) % n) for i in range(n)])  14 us
    all_to_all x2, starting transfers between devices, exchange(): return lax.all_to_all(copies, 'x', 0, 0).reshape(-1, *block.shape[1:])  7.81 us
    pallas_call x1, Pallas kernels, place(): pl.pallas_call(functools.partial(place_kernel, parts), grid=(rows // tile...  4.72 us
  transfers between devices with their start and end apart: 5, of which 3 were waited for; matrix products, arithmetic and copies ran while one was open for 3% of the time, Pallas kernels for 3%

profile of v2, /device:TPU:1, one launch (start us, length us, event | category | flops | bytes accessed | tf_op | source)
XLA Modules:
  0.0 142.7 jit_solution(8157197676248288659)
XLA Ops:
  0.6 2.8 %fusion.9 = (bf16[128,8,128]{2,0,1:T(8,128)(2,1)S(1)}, f32[128,8,128]{2,0,1:T(8,128)}) fusion(f32[128,8,128]{2,1,0:T(8,128)} %param.7, bf16[128,8,128]{2,1,0:T(8,128)(2,1)} %param.5, f32[128,8,128]{2,1,0:T(8,128)} %param.6, f32[128,8,128]{2,1,0:T(8,128)} %param.4), kind=kLoop, calls=%fused_computation.17 | loop fusion | flops 2097152 | bytes 2621440 | tf_op jit(solution)/shard_map/convert_element_type | solution.py:102
  3.4 23.0 %all_to_all.25 = bf16[128,8,128]{2,0,1:T(8,128)(2,1)S(1)} all-to-all(bf16[128,8,128]{2,0,1:T(8,128)(2,1)S(1)} %get-tuple-element.14), channel_id=1, replica_groups=mesh['x'=4,'h'=4,'fsdp'=8,'tensor'=8] {'tensor'}, dimensions={1} | all-to-all | bytes 524288 | tf_op jit(solution)/shard_map/all_to_all | solution.py:101
  26.5 11.9 %collective-permute-start.1 = (bf16[1,1024,128]{2,1,0:T(8,128)(2,1)S(1)}, bf16[1,1024,128]{2,1,0:T(8,128)(2,1)S(1)}, u32[]{:S(2)}, u32[]{:S(2)}) collective-permute-start(bf16[1,1024,128]{2,1,0:T(8,128)(2,1)S(1)} %bitcast.14), channel_id=1, source_target_pairs={{0,192},{64,0},{128,64},{192,128},{1,193},{65,1},{129,65},{193,129... | collective-permute-start | bytes 786440 | tf_op jit(solution)/shard_map/ppermute | solution.py:24
  38.4 2.1 %collective-permute-start = (bf16[1,1024,128]{2,1,0:T(8,128)(2,1)S(1)}, bf16[1,1024,128]{2,1,0:T(8,128)(2,1)S(1)}, u32[]{:S(2)}, u32[]{:S(2)}) collective-permute-start(bf16[1,1024,128]{2,1,0:T(8,128)(2,1)S(1)} %bitcast.15), channel_id=1, source_target_pairs={{0,64},{64,128},{128,192},{192,0},{1,65},{65,129},{129,193},{193,1... | collective-permute-start | bytes 786440 | tf_op jit(solution)/shard_map/ppermute | solution.py:24
  40.5 12.2 %all_gather.7 = bf16[4,512,128]{2,1,0:T(8,128)(2,1)} all-gather(bf16[1,512,128]{2,1,0:T(8,128)(2,1)S(1)} %get-tuple-element.16), channel_id=1, replica_groups=mesh['x'=4,'h'=4,'fsdp'=8,'tensor'=8] {'x'}, dimensions={0}, use_global_device_ids=true | all-gather | bytes 655360 | tf_op jit(solution)/shard_map/all_gather | solution.py:107
  52.7 11.2 %all_gather.6 = bf16[4,512,128]{2,1,0:T(8,128)(2,1)} all-gather(bf16[1,512,128]{2,1,0:T(8,128)(2,1)S(1)} %get-tuple-element.17), channel_id=1, replica_groups=mesh['x'=4,'h'=4,'fsdp'=8,'tensor'=8] {'x'}, dimensions={0}, use_global_device_ids=true | all-gather | bytes 655360 | tf_op jit(solution)/shard_map/all_gather | solution.py:107
  63.8 15.0 %collective-permute-done.1 = bf16[1,1024,128]{2,1,0:T(8,128)(2,1)S(1)} collective-permute-done((bf16[1,1024,128]{2,1,0:T(8,128)(2,1)S(1)}, bf16[1,1024,128]{2,1,0:T(8,128)(2,1)S(1)}, u32[]{:S(2)}, u32[]{:S(2)}) %collective-permute-start.1) | collective-permute-done | bytes 262176 | tf_op jit(solution)/shard_map/ppermute | solution.py:24
  78.8 0.0 collective-permute-done
  78.8 0.1 pad_maximum_fusion.1
  78.9 1.6 %broadcast_in_dim.21 = bf16[4,2,1024,128]{3,2,1,0:T(8,128)(2,1)} broadcast(bf16[2,1024,128]{2,1,0:T(8,128)(2,1)S(1)} %pad_maximum_fusion.1), dimensions={1,2,3} | broadcast | bytes 2621440 | tf_op jit(solution)/shard_map/broadcast_in_dim | solution.py:95
  80.5 3.6 %all-to-all-start.1 = ((bf16[4,2,1024,128]{3,2,1,0:T(8,128)(2,1)}), bf16[4,2,1024,128]{3,2,1,0:T(8,128)(2,1)S(1)}, u32[]{:S(2)}, u32[]{:S(2)}) async-start(bf16[4,2,1024,128]{3,2,1,0:T(8,128)(2,1)} %broadcast_in_dim.21), calls=%async_computation.1 | async-start | bytes 4194304 | tf_op jit(solution)/shard_map/all_to_all | solution.py:96
  84.1 17.8 %collective-permute-start.2 = (bf16[1,1024,128]{2,1,0:T(8,128)(2,1)S(1)}, bf16[1,1024,128]{2,1,0:T(8,128)(2,1)S(1)}, u32[]{:S(2)}, u32[]{:S(2)}) collective-permute-start(bf16[1,1024,128]{2,1,0:T(8,128)(2,1)S(1)} %broadcast_select_fusion), channel_id=1, source_target_pairs={{0,64},{1,193},{2,66},{3,195},{4,68},{5,197},{6,70},{7,199},{64,12... | collective-permute-start | bytes 786440 | tf_op jit(solution)/shard_map/ppermute | solution.py:35
  102.0 21.2 %collective-permute-done.2 = bf16[1,1024,128]{2,1,0:T(8,128)(2,1)S(1)} collective-permute-done((bf16[1,1024,128]{2,1,0:T(8,128)(2,1)S(1)}, bf16[1,1024,128]{2,1,0:T(8,128)(2,1)S(1)}, u32[]{:S(2)}, u32[]{:S(2)}) %collective-permute-start.2) | collective-permute-done | bytes 262176 | tf_op jit(solution)/shard_map/ppermute | solution.py:35
  123.2 0.0 all-to-all-done.1
  123.2 0.0 copy-start
  123.2 1.3 broadcast_in_dim.23
  124.4 4.2 %all-to-all-start.2 = ((bf16[4,1,1024,128]{3,2,1,0:T(8,128)(2,1)}), bf16[4,1,1024,128]{3,2,1,0:T(8,128)(2,1)S(1)}, u32[]{:S(2)}, u32[]{:S(2)}) async-start(bf16[4,1,1024,128]{3,2,1,0:T(8,128)(2,1)} %broadcast_in_dim.23), calls=%async_computation.2 | async-start | bytes 2097152 | tf_op jit(solution)/shard_map/all_to_all | solution.py:96
  128.6 2.1 %copy.12 = f32[128,8,128]{2,1,0:T(8,128)} copy(f32[128,8,128]{2,0,1:T(8,128)} %get-tuple-element.15) | data formatting | bytes 1048576
  130.8 0.0 copy-done
  130.8 2.3 %pad_maximum_fusion.refs_0_ = bf16[4,1024,128]{2,1,0:T(8,128)(2,1)} fusion(bf16[4,512,128]{2,1,0:T(8,128)(2,1)} %all_gather.7, bf16[4,512,128]{2,1,0:T(8,128)(2,1)} %all_gather.6), kind=kLoop, calls=%fused_computation | loop fusion | flops 2097152 | bytes 2097152 | tf_op jit(solution)/shard_map/concatenate | solution.py:114
  133.0 4.7 %shard_map.59.base = bf16[1024,2048]{1,0:T(8,128)(2,1)} custom-call(bf16[4,1024,128]{2,1,0:T(8,128)(2,1)} %pad_maximum_fusion.refs_0_, bf16[8,1024,128]{2,1,0:T(8,128)(2,1)} %bitcast.11), custom_call_target="tpu_custom_call" | custom-call | bytes 8388608 | tf_op jit(solution)/shard_map/pallas_call | solution.py:48
  137.8 0.6 all-to-all-done.2
  138.4 0.0 copy-start.1
  138.4 1.0 copy-done.1
  139.4 3.4 %shard_map.60 = bf16[1024,2048]{1,0:T(8,128)(2,1)} custom-call(s32[1]{0:T(128)} %bitcast.col, bf16[4,1024,128]{2,1,0:T(8,128)(2,1)} %bitcast.12, bf16[1024,2048]{1,0:T(8,128)(2,1)} %shard_map.59.base), custom_call_target="tpu_custom_call", output_to_operand_aliasing={{}: (2, {})} | custom-call | bytes 2097152 | tf_op jit(solution)/shard_map/pallas_call | solution.py:70
  (2 shorter events, 0.0 us)
Async XLA Ops:
  26.5 52.3 %collective-permute-start.1 = (bf16[1,1024,128]{2,1,0:T(8,128)(2,1)S(1)}, bf16[1,1024,128]{2,1,0:T(8,128)(2,1)S(1)}, u32[]{:S(2)}, u32[]{:S(2)}) collective-permute-start(bf16[1,1024,128]{2,1,0:T(8,128)(2,1)S(1)} %bitcast.14), channel_id=1, source_target_pairs={{0,192},{64,0},{128,64},{192,128},{1,193},{65,1},{129,65},{193,129... | collective-permute-start | bytes 786440 | tf_op jit(solution)/shard_map/ppermute | solution.py:24
  38.4 40.4 %collective-permute-start = (bf16[1,1024,128]{2,1,0:T(8,128)(2,1)S(1)}, bf16[1,1024,128]{2,1,0:T(8,128)(2,1)S(1)}, u32[]{:S(2)}, u32[]{:S(2)}) collective-permute-start(bf16[1,1024,128]{2,1,0:T(8,128)(2,1)S(1)} %bitcast.15), channel_id=1, source_target_pairs={{0,64},{64,128},{128,192},{192,0},{1,65},{65,129},{129,193},{193,1... | collective-permute-start | bytes 786440 | tf_op jit(solution)/shard_map/ppermute | solution.py:24
  80.5 42.7 %all-to-all-start.1 = ((bf16[4,2,1024,128]{3,2,1,0:T(8,128)(2,1)}), bf16[4,2,1024,128]{3,2,1,0:T(8,128)(2,1)S(1)}, u32[]{:S(2)}, u32[]{:S(2)}) async-start(bf16[4,2,1024,128]{3,2,1,0:T(8,128)(2,1)} %broadcast_in_dim.21), calls=%async_computation.1 | async-start | bytes 4194304 | tf_op jit(solution)/shard_map/all_to_all | solution.py:96
  84.1 39.0 %collective-permute-start.2 = (bf16[1,1024,128]{2,1,0:T(8,128)(2,1)S(1)}, bf16[1,1024,128]{2,1,0:T(8,128)(2,1)S(1)}, u32[]{:S(2)}, u32[]{:S(2)}) collective-permute-start(bf16[1,1024,128]{2,1,0:T(8,128)(2,1)S(1)} %broadcast_select_fusion), channel_id=1, source_target_pairs={{0,64},{1,193},{2,66},{3,195},{4,68},{5,197},{6,70},{7,199},{64,12... | collective-permute-start | bytes 786440 | tf_op jit(solution)/shard_map/ppermute | solution.py:35
  123.2 7.6 %copy-start = (bf16[4,2,1024,128]{3,2,1,0:T(8,128)(2,1)}, bf16[4,2,1024,128]{3,2,1,0:T(8,128)(2,1)S(1)}, u32[]{:S(2)}) copy-start(bf16[4,2,1024,128]{3,2,1,0:T(8,128)(2,1)S(1)} %all-to-all-done.1) | copy-start | bytes 6291460
  124.4 13.9 %all-to-all-start.2 = ((bf16[4,1,1024,128]{3,2,1,0:T(8,128)(2,1)}), bf16[4,1,1024,128]{3,2,1,0:T(8,128)(2,1)S(1)}, u32[]{:S(2)}, u32[]{:S(2)}) async-start(bf16[4,1,1024,128]{3,2,1,0:T(8,128)(2,1)} %broadcast_in_dim.23), calls=%async_computation.2 | async-start | bytes 2097152 | tf_op jit(solution)/shard_map/all_to_all | solution.py:96
  138.4 1.0 copy-start.1

commit v3 on v2

v3 whole, which is shorter than its diff:
```python
import functools
import jax
import jax.numpy as jnp
from jax import lax
from jax.sharding import Mesh, PartitionSpec as P
from jax.experimental import pallas as pl
from jax.experimental.pallas import tpu as pltpu

NX, NH, LANES = 4, 4, 128


def adamw_update(master, gradient, first_moment, second_moment):
    grad_full = gradient.astype(jnp.float32)
    moment_one = 0.9 * first_moment + 0.1 * grad_full
    moment_two = 0.95 * second_moment + 0.05 * grad_full * grad_full
    corr_one = 1.0 - 0.9**10
    corr_two = 1.0 - 0.95**10
    step_size = moment_one / corr_one / (jnp.sqrt(moment_two / corr_two) + 1e-08)
    return master * (1.0 - 0.1 * 0.1) - 0.1 * step_size


def swap_z(block, sign):
    n = lax.axis_size("tensor")
    pairs = [
        (h * n + t, (h + (sign if t % 2 == 0 else -sign)) % NH * n + t)
        for h in range(NH)
        for t in range(n)
    ]
    return lax.ppermute(block, ("h", "tensor"), pairs)


def place_kernel(parts, *refs):
    out = refs[-1]
    h = lax.axis_index("h")
    sign = 1 - 2 * lax.rem(lax.axis_index("tensor"), 2)
    for ref, steps in zip(refs[:-1], parts):
        for x in range(NX):
            for k, step in enumerate(steps):
                col = lax.rem(h - sign * step + NH, NH) + NH * x
                out[:, pl.ds(pl.multiple_of(col * LANES, LANES), LANES)] = ref[
                    x * len(steps) + k
                ]


def place(blocks, parts, rows, tile=256):
    return pl.pallas_call(
        functools.partial(place_kernel, parts),
        grid=(rows // tile,),
        out_shape=jax.ShapeDtypeStruct((rows, NX * NH * LANES), jnp.bfloat16),
        in_specs=[
            pl.BlockSpec((NX * len(p), tile, LANES), lambda i: (0, i, 0)) for p in parts
        ],
        out_specs=pl.BlockSpec((tile, NX * NH * LANES), lambda i: (i, 0)),
        compiler_params=pltpu.CompilerParams(vmem_limit_bytes=8 << 20),
        cost_estimate=pl.CostEstimate(
            flops=0, bytes_accessed=rows * NX * NH * LANES * 4, transcendentals=0
        ),
    )(*blocks)


def insert_kernel(block, base, out, sems):
    del base
    h = lax.rem(lax.axis_index("h") + 2, NH)
    copies = [
        pltpu.make_async_copy(
            block.at[x],
            out.at[:, pl.ds(pl.multiple_of((h + NH * x) * LANES, LANES), LANES)],
            sems.at[x],
        )
        for x in range(NX)
    ]
    for c in copies:
        c.start()
    for c in copies:
        c.wait()


def insert(rollout, block):
    return pl.pallas_call(
        insert_kernel,
        in_specs=[
            pl.BlockSpec(memory_space=pltpu.VMEM),
            pl.BlockSpec(memory_space=pl.ANY),
        ],
        out_specs=pl.BlockSpec(memory_space=pl.ANY),
        out_shape=jax.ShapeDtypeStruct(rollout.shape, rollout.dtype),
        scratch_shapes=[pltpu.SemaphoreType.DMA((NX,))],
        input_output_aliases={1: 0},
        compiler_params=pltpu.CompilerParams(vmem_limit_bytes=4 << 20),
        cost_estimate=pl.CostEstimate(
            flops=0, bytes_accessed=4 * block.size, transcendentals=0
        ),
    )(block, rollout)


def exchange(block):
    copies = jnp.broadcast_to(block[None], (NX, *block.shape))
    return lax.all_to_all(copies, "x", 0, 0).reshape(-1, *block.shape[1:])


def on_device(master, gradient, first_moment, second_moment):
    new_master = adamw_update(master, gradient, first_moment, second_moment)
    own = lax.all_to_all(
        new_master.astype(jnp.bfloat16), "tensor", split_axis=1, concat_axis=0, tiled=True
    )
    rows = own.shape[0]
    own = own.reshape(1, rows, LANES)
    one, other = swap_z(own, 1), swap_z(own, -1)
    halves = [
        lax.all_gather(part, "x", axis=0, tiled=True)
        for part in jnp.split(own, 2, axis=1)
    ]
    own = jnp.concatenate(halves, axis=1)
    one, own = lax.optimization_barrier((one, own))
    far = swap_z(one, 1)
    near = exchange(jnp.concatenate([one, other]))
    rollout = place([own, near], [(0,), (1, -1)], rows)
    far, near = lax.optimization_barrier((far, near))
    rollout = insert(rollout, exchange(far))
    return (new_master, rollout[:, None, :])


def solution(mesh):
    grid = mesh.devices
    fine = Mesh(
        grid.reshape(NX, NH, *grid.shape[1:]), ("x", "h", *mesh.axis_names[1:])
    )
    placed = P(("fsdp", "tensor"), None, ("x", "h"))
    return jax.shard_map(
        on_device,
        mesh=fine,
        in_specs=(placed,) * 4,
        out_specs=(placed, P("fsdp", "tensor", None)),
        check_vma=False,
    )
```

time: 146 us -> 146 us (level); the launches traced: 143 us -> 145 us
  waiting for transfers between devices: 36.8 us -> 45.2 us
  Pallas kernels: 8.07 us -> 5.15 us
  other arithmetic: 5.11 us -> 2.89 us
    all_to_all x2, waiting for transfers between devices: 0.63 us -> 10.3 us  [exchange(): return lax.all_to_all(copies, 'x', 0, 0).reshape(-1, *block.shape[1:])]
    all_to_all x2, starting transfers between devices: 7.81 us -> 13.8 us  [exchange(): return lax.all_to_all(copies, 'x', 0, 0).reshape(-1, *block.shape[1:])]
    ppermute x3, starting transfers between devices: 31.8 us -> 26.5 us  [swap_z(): return lax.ppermute(block, ('h', 'tensor'), pairs)]
    concatenate x1, other arithmetic: 2.26 us -> 0.07 us  [on_device(): own = jnp.concatenate(halves, axis=1)]
    pallas_call x1, Pallas kernels: 4.72 us -> 2.93 us  [place(): pl.pallas_call(functools.partial(place_kernel, parts), grid=(rows // tile...]
    unnamed x5 -> x3, local copies, waits for them, and re-layouts: 3.12 us -> 2.84 us
  transfers between devices with their start and end apart: 5 -> 5, of which waited for: 3 -> 3; matrix products, arithmetic and copies ran while one was open for 3% -> 2% of each run, Pallas kernels for 3% -> 2%
where the time goes in v3:
time: 146 us; the launch traced here: 145 us
  blocking collectives  45.6 us (31%)
  waiting for transfers between devices  45.2 us (31%)
  starting transfers between devices  40.3 us (28%)
  local copies, waits for them, and re-layouts  5.61 us (4%)
  Pallas kernels  5.15 us (4%)
  other arithmetic  2.89 us (2%)
    ppermute x3, waiting for transfers between devices, swap_z(): return lax.ppermute(block, ('h', 'tensor'), pairs)  34.9 us
    ppermute x3, starting transfers between devices, swap_z(): return lax.ppermute(block, ('h', 'tensor'), pairs)  26.5 us
    all_to_all x1, blocking collectives, on_device(): lax.all_to_all(new_master.astype(jnp.bfloat16), 'tensor', split_axis=1, c...  23 us
    all_gather x2, blocking collectives, on_device(): lax.all_gather(part, 'x', axis=0, tiled=True)  22.5 us
    all_to_all x2, starting transfers between devices, exchange(): return lax.all_to_all(copies, 'x', 0, 0).reshape(-1, *block.shape[1:])  13.8 us
    all_to_all x2, waiting for transfers between devices, exchange(): return lax.all_to_all(copies, 'x', 0, 0).reshape(-1, *block.shape[1:])  10.3 us
    pallas_call x1, Pallas kernels, place(): pl.pallas_call(functools.partial(place_kernel, parts), grid=(rows // tile...  2.93 us
  transfers between devices with their start and end apart: 5, of which 3 were waited for; matrix products, arithmetic and copies ran while one was open for 2% of the time, Pallas kernels for 2%

profile of v3, /device:TPU:1, one launch (start us, length us, event | category | flops | bytes accessed | tf_op | source)
XLA Modules:
  0.0 145.3 jit_solution(5300039870065373745)
XLA Ops:
  0.6 2.8 %fusion.9 = (bf16[128,8,128]{2,0,1:T(8,128)(2,1)S(1)}, f32[128,8,128]{2,0,1:T(8,128)}) fusion(f32[128,8,128]{2,1,0:T(8,128)} %param.7, bf16[128,8,128]{2,1,0:T(8,128)(2,1)} %param.5, f32[128,8,128]{2,1,0:T(8,128)} %param.6, f32[128,8,128]{2,1,0:T(8,128)} %param.4), kind=kLoop, calls=%fused_computation.16 | loop fusion | flops 2097152 | bytes 2621440 | tf_op jit(solution)/shard_map/convert_element_type | solution.py:104
  3.4 23.0 %all_to_all.25 = bf16[128,8,128]{2,0,1:T(8,128)(2,1)S(1)} all-to-all(bf16[128,8,128]{2,0,1:T(8,128)(2,1)S(1)} %get-tuple-element.10), channel_id=1, replica_groups=mesh['x'=4,'h'=4,'fsdp'=8,'tensor'=8] {'tensor'}, dimensions={1} | all-to-all | bytes 524288 | tf_op jit(solution)/shard_map/all_to_all | solution.py:103
  26.5 4.7 %collective-permute-start.2 = (bf16[1,1024,128]{2,1,0:T(8,128)(2,1)S(1)}, bf16[1,1024,128]{2,1,0:T(8,128)(2,1)S(1)}, u32[]{:S(2)}, u32[]{:S(2)}) collective-permute-start(bf16[1,1024,128]{2,1,0:T(8,128)(2,1)S(1)} %bitcast.12), channel_id=1, source_target_pairs={{0,192},{1,65},{2,194},{3,67},{4,196},{5,69},{6,198},{7,71},{64,0}... | collective-permute-start | bytes 786440 | tf_op jit(solution)/shard_map/ppermute | solution.py:29
  31.1 9.3 %collective-permute-start = (bf16[1,1024,128]{2,1,0:T(8,128)(2,1)S(1)}, bf16[1,1024,128]{2,1,0:T(8,128)(2,1)S(1)}, u32[]{:S(2)}, u32[]{:S(2)}) collective-permute-start(bf16[1,1024,128]{2,1,0:T(8,128)(2,1)S(1)} %bitcast.13), channel_id=1, source_target_pairs={{0,64},{1,193},{2,66},{3,195},{4,68},{5,197},{6,70},{7,199},{64,12... | collective-permute-start | bytes 786440 | tf_op jit(solution)/shard_map/ppermute | solution.py:29
  40.5 11.7 %all_gather.6 = bf16[4,512,128]{2,1,0:T(8,128)(2,1)S(1)} all-gather(bf16[1,512,128]{2,1,0:T(8,128)(2,1)S(1)} %get-tuple-element.12), channel_id=1, replica_groups=mesh['x'=4,'h'=4,'fsdp'=8,'tensor'=8] {'x'}, dimensions={0}, use_global_device_ids=true | all-gather | bytes 655360 | tf_op jit(solution)/shard_map/all_gather | solution.py:110
  52.2 10.8 %all_gather.7 = bf16[4,512,128]{2,1,0:T(8,128)(2,1)S(1)} all-gather(bf16[1,512,128]{2,1,0:T(8,128)(2,1)S(1)} %get-tuple-element.13), channel_id=1, replica_groups=mesh['x'=4,'h'=4,'fsdp'=8,'tensor'=8] {'x'}, dimensions={0}, use_global_device_ids=true | all-gather | bytes 655360 | tf_op jit(solution)/shard_map/all_gather | solution.py:110
  63.0 0.1 pad_maximum_fusion.refs_0_
  63.1 17.0 %collective-permute-done = bf16[1,1024,128]{2,1,0:T(8,128)(2,1)S(1)} collective-permute-done((bf16[1,1024,128]{2,1,0:T(8,128)(2,1)S(1)}, bf16[1,1024,128]{2,1,0:T(8,128)(2,1)S(1)}, u32[]{:S(2)}, u32[]{:S(2)}) %collective-permute-start) | collective-permute-done | bytes 262176 | tf_op jit(solution)/shard_map/ppermute | solution.py:29
  80.0 0.0 copy-start
  80.1 0.0 collective-permute-done.2
  80.1 0.7 copy-done
  80.8 0.1 pad_maximum_fusion.1
  80.8 1.6 %broadcast_in_dim.8 = bf16[4,2,1024,128]{3,2,1,0:T(8,128)(2,1)} broadcast(bf16[2,1024,128]{2,1,0:T(8,128)(2,1)S(1)} %pad_maximum_fusion.1), dimensions={1,2,3} | broadcast | bytes 2621440 | tf_op jit(solution)/shard_map/broadcast_in_dim | solution.py:97
  82.4 9.5 %all-to-all-start.1 = ((bf16[4,2,1024,128]{3,2,1,0:T(8,128)(2,1)}), bf16[4,2,1024,128]{3,2,1,0:T(8,128)(2,1)S(1)}, u32[]{:S(2)}, u32[]{:S(2)}) async-start(bf16[4,2,1024,128]{3,2,1,0:T(8,128)(2,1)} %broadcast_in_dim.8), calls=%async_computation.1 | async-start | bytes 4194304 | tf_op jit(solution)/shard_map/all_to_all | solution.py:98
  91.9 12.5 %collective-permute-start.1 = (bf16[1,1024,128]{2,1,0:T(8,128)(2,1)}, bf16[1,1024,128]{2,1,0:T(8,128)(2,1)S(1)}, u32[]{:S(2)}, u32[]{:S(2)}) collective-permute-start(bf16[1,1024,128]{2,1,0:T(8,128)(2,1)} %copy-done), channel_id=1, source_target_pairs={{0,64},{1,193},{2,66},{3,195},{4,68},{5,197},{6,70},{7,199},{64,12... | collective-permute-start | bytes 786440 | tf_op jit(solution)/shard_map/ppermute | solution.py:29
  104.4 17.9 %collective-permute-done.1 = bf16[1,1024,128]{2,1,0:T(8,128)(2,1)S(1)} collective-permute-done((bf16[1,1024,128]{2,1,0:T(8,128)(2,1)}, bf16[1,1024,128]{2,1,0:T(8,128)(2,1)S(1)}, u32[]{:S(2)}, u32[]{:S(2)}) %collective-permute-start.1) | collective-permute-done | bytes 262176 | tf_op jit(solution)/shard_map/ppermute | solution.py:29
  122.3 0.0 all-to-all-done.1
  122.3 1.2 broadcast_in_dim.19
  123.5 4.2 %all-to-all-start.2 = ((bf16[4,1,1024,128]{3,2,1,0:T(8,128)(2,1)}), bf16[4,1,1024,128]{3,2,1,0:T(8,128)(2,1)}, u32[]{:S(2)}, u32[]{:S(2)}) async-start(bf16[4,1,1024,128]{3,2,1,0:T(8,128)(2,1)} %broadcast_in_dim.19), calls=%async_computation.2 | async-start | bytes 2097152 | tf_op jit(solution)/shard_map/all_to_all | solution.py:98
  127.7 2.1 %copy.12 = f32[128,8,128]{2,1,0:T(8,128)} copy(f32[128,8,128]{2,0,1:T(8,128)} %get-tuple-element.11) | data formatting | bytes 1048576
  129.9 2.9 %shard_map.59.base = bf16[1024,2048]{1,0:T(8,128)(2,1)} custom-call(bf16[4,1024,128]{2,1,0:T(8,128)(2,1)S(1)} %pad_maximum_fusion.refs_0_, bf16[8,1024,128]{2,1,0:T(8,128)(2,1)S(1)} %bitcast.9), custom_call_target="tpu_custom_call" | custom-call | bytes 8388608 | tf_op jit(solution)/shard_map/pallas_call | solution.py:46
  132.8 10.3 %all-to-all-done.2 = bf16[4,1,1024,128]{3,2,1,0:T(8,128)(2,1)} async-done(((bf16[4,1,1024,128]{3,2,1,0:T(8,128)(2,1)}), bf16[4,1,1024,128]{3,2,1,0:T(8,128)(2,1)}, u32[]{:S(2)}, u32[]{:S(2)}) %all-to-all-start.2) | async-done | bytes 1048608 | tf_op jit(solution)/shard_map/all_to_all | solution.py:98
  143.1 2.2 %shard_map.60 = bf16[1024,2048]{1,0:T(8,128)(2,1)} custom-call(bf16[4,1024,128]{2,1,0:T(8,128)(2,1)} %bitcast.7.block, bf16[1024,2048]{1,0:T(8,128)(2,1)} %shard_map.59.base), custom_call_target="tpu_custom_call", output_to_operand_aliasing={{}: (1, {})} | custom-call | bytes 2097152 | tf_op jit(solution)/shard_map/pallas_call | solution.py:79
  (1 shorter events, 0.0 us)
Async XLA Ops:
  26.5 53.6 %collective-permute-start.2 = (bf16[1,1024,128]{2,1,0:T(8,128)(2,1)S(1)}, bf16[1,1024,128]{2,1,0:T(8,128)(2,1)S(1)}, u32[]{:S(2)}, u32[]{:S(2)}) collective-permute-start(bf16[1,1024,128]{2,1,0:T(8,128)(2,1)S(1)} %bitcast.12), channel_id=1, source_target_pairs={{0,192},{1,65},{2,194},{3,67},{4,196},{5,69},{6,198},{7,71},{64,0}... | collective-permute-start | bytes 786440 | tf_op jit(solution)/shard_map/ppermute | solution.py:29
  31.1 48.9 %collective-permute-start = (bf16[1,1024,128]{2,1,0:T(8,128)(2,1)S(1)}, bf16[1,1024,128]{2,1,0:T(8,128)(2,1)S(1)}, u32[]{:S(2)}, u32[]{:S(2)}) collective-permute-start(bf16[1,1024,128]{2,1,0:T(8,128)(2,1)S(1)} %bitcast.13), channel_id=1, source_target_pairs={{0,64},{1,193},{2,66},{3,195},{4,68},{5,197},{6,70},{7,199},{64,12... | collective-permute-start | bytes 786440 | tf_op jit(solution)/shard_map/ppermute | solution.py:29
  80.0 0.7 copy-start
  82.4 39.9 %all-to-all-start.1 = ((bf16[4,2,1024,128]{3,2,1,0:T(8,128)(2,1)}), bf16[4,2,1024,128]{3,2,1,0:T(8,128)(2,1)S(1)}, u32[]{:S(2)}, u32[]{:S(2)}) async-start(bf16[4,2,1024,128]{3,2,1,0:T(8,128)(2,1)} %broadcast_in_dim.8), calls=%async_computation.1 | async-start | bytes 4194304 | tf_op jit(solution)/shard_map/all_to_all | solution.py:98
  91.9 30.4 %collective-permute-start.1 = (bf16[1,1024,128]{2,1,0:T(8,128)(2,1)}, bf16[1,1024,128]{2,1,0:T(8,128)(2,1)S(1)}, u32[]{:S(2)}, u32[]{:S(2)}) collective-permute-start(bf16[1,1024,128]{2,1,0:T(8,128)(2,1)} %copy-done), channel_id=1, source_target_pairs={{0,64},{1,193},{2,66},{3,195},{4,68},{5,197},{6,70},{7,199},{64,12... | collective-permute-start | bytes 786440 | tf_op jit(solution)/shard_map/ppermute | solution.py:29
  123.5 19.6 %all-to-all-start.2 = ((bf16[4,1,1024,128]{3,2,1,0:T(8,128)(2,1)}), bf16[4,1,1024,128]{3,2,1,0:T(8,128)(2,1)}, u32[]{:S(2)}, u32[]{:S(2)}) async-start(bf16[4,1,1024,128]{3,2,1,0:T(8,128)(2,1)} %broadcast_in_dim.19), calls=%async_computation.2 | async-start | bytes 2097152 | tf_op jit(solution)/shard_map/all_to_all | solution.py:98

commit v4 on v3

--- a/solution.py
+++ b/solution.py
@@ -19,27 +19,29 @@
     return master * (1.0 - 0.1 * 0.1) - 0.1 * step_size
 
 
-def swap_z(block, sign):
-    n = lax.axis_size("tensor")
+def ring(axis, block, step):
+    n = lax.axis_size(axis)
+    return lax.ppermute(block, axis, [(i, (i + step) % n) for i in range(n)])
+
+
+def onward(axis, fore, back):
+    n, m = lax.axis_size(axis), lax.axis_size("tensor")
     pairs = [
-        (h * n + t, (h + (sign if t % 2 == 0 else -sign)) % NH * n + t)
-        for h in range(NH)
-        for t in range(n)
+        (i * m + t, (i + (1 if t % 2 == 0 else -1)) % n * m + t)
+        for i in range(n)
+        for t in range(m)
     ]
-    return lax.ppermute(block, ("h", "tensor"), pairs)
+    core = lax.axis_index("tensor") % 2
+    return lax.ppermute(jnp.where(core == 0, fore, back), (axis, "tensor"), pairs)
 
 
 def place_kernel(parts, *refs):
     out = refs[-1]
     h = lax.axis_index("h")
-    sign = 1 - 2 * lax.rem(lax.axis_index("tensor"), 2)
-    for ref, steps in zip(refs[:-1], parts):
-        for x in range(NX):
-            for k, step in enumerate(steps):
-                col = lax.rem(h - sign * step + NH, NH) + NH * x
-                out[:, pl.ds(pl.multiple_of(col * LANES, LANES), LANES)] = ref[
-                    x * len(steps) + k
-                ]
+    for ref, places in zip(refs[:-1], parts):
+        for k, (dx, dh) in enumerate(places):
+            col = lax.rem(h - dh + NH, NH) + NH * dx
+            out[:, pl.ds(pl.multiple_of(col * LANES, LANES), LANES)] = ref[k]
 
 
 def place(blocks, parts, rows, tile=256):
@@ -48,7 +50,7 @@
         grid=(rows // tile,),
         out_shape=jax.ShapeDtypeStruct((rows, NX * NH * LANES), jnp.bfloat16),
         in_specs=[
-            pl.BlockSpec((NX * len(p), tile, LANES), lambda i: (0, i, 0)) for p in parts
+            pl.BlockSpec((len(p), tile, LANES), lambda i: (0, i, 0)) for p in parts
         ],
         out_specs=pl.BlockSpec((tile, NX * NH * LANES), lambda i: (i, 0)),
         compiler_params=pltpu.CompilerParams(vmem_limit_bytes=8 << 20),
@@ -105,16 +107,20 @@
     )
     rows = own.shape[0]
     own = own.reshape(1, rows, LANES)
-    one, other = swap_z(own, 1), swap_z(own, -1)
     halves = [
         lax.all_gather(part, "x", axis=0, tiled=True)
         for part in jnp.split(own, 2, axis=1)
     ]
+    up, down = ring("h", own, 1), ring("h", own, -1)
+    up, down, halves = lax.optimization_barrier((up, down, halves))
+    far = onward("h", up, down)
+    near = exchange(jnp.concatenate([up, down]))
     own = jnp.concatenate(halves, axis=1)
-    one, own = lax.optimization_barrier((one, own))
-    far = swap_z(one, 1)
-    near = exchange(jnp.concatenate([one, other]))
-    rollout = place([own, near], [(0,), (1, -1)], rows)
+    parts = [
+        [(x, 0) for x in range(NX)],
+        [(x, dh) for x in range(NX) for dh in (1, -1)],
+    ]
+    rollout = place([own, near], parts, rows)
     far, near = lax.optimization_barrier((far, near))
     rollout = insert(rollout, exchange(far))
     return (new_master, rollout[:, None, :])

time: 146 us -> 142 us (0.973); the launches traced: 145 us -> 139 us
  waiting for transfers between devices: 45.2 us -> 39.6 us
    all_to_all x2, waiting for transfers between devices: 10.3 us -> 3.4 us  [exchange(): return lax.all_to_all(copies, 'x', 0, 0).reshape(-1, *block.shape[1:])]
    all_to_all x2, starting transfers between devices: 13.8 us -> 7.82 us  [exchange(): return lax.all_to_all(copies, 'x', 0, 0).reshape(-1, *block.shape[1:])]
    ppermute x3, starting transfers between devices: 26.5 us -> 31.8 us  [the longest x1 17.8 us: onward(): lax.ppermute(jnp.where(core == 0, fore, back), (axis, 'tensor'), pairs)]
where the time goes in v4:
time: 142 us; the launch traced here: 139 us
  blocking collectives  46.4 us (33%)
  starting transfers between devices  39.6 us (28%)
  waiting for transfers between devices  39.6 us (28%)
  local copies, waits for them, and re-layouts  4.85 us (3%)
  other arithmetic  4.12 us (3%)
  Pallas kernels  3.93 us (3%)
    all_gather x2, blocking collectives, on_device(): lax.all_gather(part, 'x', axis=0, tiled=True)  23.4 us
    all_to_all x1, blocking collectives, on_device(): lax.all_to_all(new_master.astype(jnp.bfloat16), 'tensor', split_axis=1, c...  23 us
    ppermute x1, waiting for transfers between devices, onward(): lax.ppermute(jnp.where(core == 0, fore, back), (axis, 'tensor'), pairs)  21.2 us
    ppermute x1, starting transfers between devices, onward(): lax.ppermute(jnp.where(core == 0, fore, back), (axis, 'tensor'), pairs)  17.8 us
    ppermute x2, waiting for transfers between devices, ring(): return lax.ppermute(block, axis, [(i, (i + step) % n) for i in range(n)])  15 us
    ppermute x2, starting transfers between devices, ring(): return lax.ppermute(block, axis, [(i, (i + step) % n) for i in range(n)])  14 us
    all_to_all x2, starting transfers between devices, exchange(): return lax.all_to_all(copies, 'x', 0, 0).reshape(-1, *block.shape[1:])  7.82 us
    all_to_all x2, waiting for transfers between devices, exchange(): return lax.all_to_all(copies, 'x', 0, 0).reshape(-1, *block.shape[1:])  3.4 us
  transfers between devices with their start and end apart: 5, of which 3 were waited for; matrix products, arithmetic and copies ran while one was open for 2% of the time, Pallas kernels for 2%

profile of v4, /device:TPU:1, one launch (start us, length us, event | category | flops | bytes accessed | tf_op | source)
XLA Modules:
  0.0 139.2 jit_solution(6013294042047814496)
XLA Ops:
  0.6 2.8 %fusion.9 = (bf16[128,8,128]{2,0,1:T(8,128)(2,1)S(1)}, f32[128,8,128]{2,0,1:T(8,128)}) fusion(f32[128,8,128]{2,1,0:T(8,128)} %param.7, bf16[128,8,128]{2,1,0:T(8,128)(2,1)} %param.5, f32[128,8,128]{2,1,0:T(8,128)} %param.6, f32[128,8,128]{2,1,0:T(8,128)} %param.4), kind=kLoop, calls=%fused_computation.17 | loop fusion | flops 2097152 | bytes 2621440 | tf_op jit(solution)/shard_map/convert_element_type | solution.py:106
  3.4 23.0 %all_to_all.25 = bf16[128,8,128]{2,0,1:T(8,128)(2,1)S(1)} all-to-all(bf16[128,8,128]{2,0,1:T(8,128)(2,1)S(1)} %get-tuple-element.14), channel_id=1, replica_groups=mesh['x'=4,'h'=4,'fsdp'=8,'tensor'=8] {'tensor'}, dimensions={1} | all-to-all | bytes 524288 | tf_op jit(solution)/shard_map/all_to_all | solution.py:105
  26.5 11.9 %collective-permute-start.1 = (bf16[1,1024,128]{2,1,0:T(8,128)(2,1)S(1)}, bf16[1,1024,128]{2,1,0:T(8,128)(2,1)S(1)}, u32[]{:S(2)}, u32[]{:S(2)}) collective-permute-start(bf16[1,1024,128]{2,1,0:T(8,128)(2,1)S(1)} %bitcast.13), channel_id=1, source_target_pairs={{0,192},{64,0},{128,64},{192,128},{1,193},{65,1},{129,65},{193,129... | collective-permute-start | bytes 786440 | tf_op jit(solution)/shard_map/ppermute | solution.py:24
  38.4 2.1 %collective-permute-start = (bf16[1,1024,128]{2,1,0:T(8,128)(2,1)S(1)}, bf16[1,1024,128]{2,1,0:T(8,128)(2,1)S(1)}, u32[]{:S(2)}, u32[]{:S(2)}) collective-permute-start(bf16[1,1024,128]{2,1,0:T(8,128)(2,1)S(1)} %bitcast.14), channel_id=1, source_target_pairs={{0,64},{64,128},{128,192},{192,0},{1,65},{65,129},{129,193},{193,1... | collective-permute-start | bytes 786440 | tf_op jit(solution)/shard_map/ppermute | solution.py:24
  40.5 12.2 %all_gather.7 = bf16[4,512,128]{2,1,0:T(8,128)(2,1)} all-gather(bf16[1,512,128]{2,1,0:T(8,128)(2,1)S(1)} %get-tuple-element.16), channel_id=1, replica_groups=mesh['x'=4,'h'=4,'fsdp'=8,'tensor'=8] {'x'}, dimensions={0}, use_global_device_ids=true | all-gather | bytes 655360 | tf_op jit(solution)/shard_map/all_gather | solution.py:111
  52.7 11.2 %all_gather.6 = bf16[4,512,128]{2,1,0:T(8,128)(2,1)} all-gather(bf16[1,512,128]{2,1,0:T(8,128)(2,1)S(1)} %get-tuple-element.17), channel_id=1, replica_groups=mesh['x'=4,'h'=4,'fsdp'=8,'tensor'=8] {'x'}, dimensions={0}, use_global_device_ids=true | all-gather | bytes 655360 | tf_op jit(solution)/shard_map/all_gather | solution.py:111
  63.8 15.0 %collective-permute-done.1 = bf16[1,1024,128]{2,1,0:T(8,128)(2,1)S(1)} collective-permute-done((bf16[1,1024,128]{2,1,0:T(8,128)(2,1)S(1)}, bf16[1,1024,128]{2,1,0:T(8,128)(2,1)S(1)}, u32[]{:S(2)}, u32[]{:S(2)}) %collective-permute-start.1) | collective-permute-done | bytes 262176 | tf_op jit(solution)/shard_map/ppermute | solution.py:24
  78.8 0.0 collective-permute-done
  78.8 0.1 pad_maximum_fusion.1
  78.9 1.6 %broadcast_in_dim.8 = bf16[4,2,1024,128]{3,2,1,0:T(8,128)(2,1)} broadcast(bf16[2,1024,128]{2,1,0:T(8,128)(2,1)S(1)} %pad_maximum_fusion.1), dimensions={1,2,3} | broadcast | bytes 2621440 | tf_op jit(solution)/shard_map/broadcast_in_dim | solution.py:99
  80.5 3.6 %all-to-all-start.1 = ((bf16[4,2,1024,128]{3,2,1,0:T(8,128)(2,1)}), bf16[4,2,1024,128]{3,2,1,0:T(8,128)(2,1)S(1)}, u32[]{:S(2)}, u32[]{:S(2)}) async-start(bf16[4,2,1024,128]{3,2,1,0:T(8,128)(2,1)} %broadcast_in_dim.8), calls=%async_computation.1 | async-start | bytes 4194304 | tf_op jit(solution)/shard_map/all_to_all | solution.py:100
  84.1 17.8 %collective-permute-start.2 = (bf16[1,1024,128]{2,1,0:T(8,128)(2,1)S(1)}, bf16[1,1024,128]{2,1,0:T(8,128)(2,1)S(1)}, u32[]{:S(2)}, u32[]{:S(2)}) collective-permute-start(bf16[1,1024,128]{2,1,0:T(8,128)(2,1)S(1)} %broadcast_select_fusion), channel_id=1, source_target_pairs={{0,64},{1,193},{2,66},{3,195},{4,68},{5,197},{6,70},{7,199},{64,12... | collective-permute-start | bytes 786440 | tf_op jit(solution)/shard_map/ppermute | solution.py:35
  102.0 21.2 %collective-permute-done.2 = bf16[1,1024,128]{2,1,0:T(8,128)(2,1)S(1)} collective-permute-done((bf16[1,1024,128]{2,1,0:T(8,128)(2,1)S(1)}, bf16[1,1024,128]{2,1,0:T(8,128)(2,1)S(1)}, u32[]{:S(2)}, u32[]{:S(2)}) %collective-permute-start.2) | collective-permute-done | bytes 262176 | tf_op jit(solution)/shard_map/ppermute | solution.py:35
  123.2 0.0 all-to-all-done.1
  123.2 1.1 broadcast_in_dim.19
  124.3 4.2 %all-to-all-start.2 = ((bf16[4,1,1024,128]{3,2,1,0:T(8,128)(2,1)}), bf16[4,1,1024,128]{3,2,1,0:T(8,128)(2,1)S(1)}, u32[]{:S(2)}, u32[]{:S(2)}) async-start(bf16[4,1,1024,128]{3,2,1,0:T(8,128)(2,1)} %broadcast_in_dim.19), calls=%async_computation.2 | async-start | bytes 2097152 | tf_op jit(solution)/shard_map/all_to_all | solution.py:100
  128.5 2.1 %copy.12 = f32[128,8,128]{2,1,0:T(8,128)} copy(f32[128,8,128]{2,0,1:T(8,128)} %get-tuple-element.15) | data formatting | bytes 1048576
  130.6 1.3 pad_maximum_fusion.refs_0_
  131.9 2.9 %shard_map.59.base = bf16[1024,2048]{1,0:T(8,128)(2,1)} custom-call(bf16[4,1024,128]{2,1,0:T(8,128)(2,1)S(1)} %pad_maximum_fusion.refs_0_, bf16[8,1024,128]{2,1,0:T(8,128)(2,1)S(1)} %bitcast.9), custom_call_target="tpu_custom_call" | custom-call | bytes 8388608 | tf_op jit(solution)/shard_map/pallas_call | solution.py:48
  134.8 3.4 %all-to-all-done.2 = bf16[4,1,1024,128]{3,2,1,0:T(8,128)(2,1)S(1)} async-done(((bf16[4,1,1024,128]{3,2,1,0:T(8,128)(2,1)}), bf16[4,1,1024,128]{3,2,1,0:T(8,128)(2,1)S(1)}, u32[]{:S(2)}, u32[]{:S(2)}) %all-to-all-start.2) | async-done | bytes 1048608 | tf_op jit(solution)/shard_map/all_to_all | solution.py:100
  138.2 1.0 shard_map.60
  (2 shorter events, 0.0 us)
Async XLA Ops:
  26.5 52.3 %collective-permute-start.1 = (bf16[1,1024,128]{2,1,0:T(8,128)(2,1)S(1)}, bf16[1,1024,128]{2,1,0:T(8,128)(2,1)S(1)}, u32[]{:S(2)}, u32[]{:S(2)}) collective-permute-start(bf16[1,1024,128]{2,1,0:T(8,128)(2,1)S(1)} %bitcast.13), channel_id=1, source_target_pairs={{0,192},{64,0},{128,64},{192,128},{1,193},{65,1},{129,65},{193,129... | collective-permute-start | bytes 786440 | tf_op jit(solution)/shard_map/ppermute | solution.py:24
  38.4 40.4 %collective-permute-start = (bf16[1,1024,128]{2,1,0:T(8,128)(2,1)S(1)}, bf16[1,1024,128]{2,1,0:T(8,128)(2,1)S(1)}, u32[]{:S(2)}, u32[]{:S(2)}) collective-permute-start(bf16[1,1024,128]{2,1,0:T(8,128)(2,1)S(1)} %bitcast.14), channel_id=1, source_target_pairs={{0,64},{64,128},{128,192},{192,0},{1,65},{65,129},{129,193},{193,1... | collective-permute-start | bytes 786440 | tf_op jit(solution)/shard_map/ppermute | solution.py:24
  80.5 42.7 %all-to-all-start.1 = ((bf16[4,2,1024,128]{3,2,1,0:T(8,128)(2,1)}), bf16[4,2,1024,128]{3,2,1,0:T(8,128)(2,1)S(1)}, u32[]{:S(2)}, u32[]{:S(2)}) async-start(bf16[4,2,1024,128]{3,2,1,0:T(8,128)(2,1)} %broadcast_in_dim.8), calls=%async_computation.1 | async-start | bytes 4194304 | tf_op jit(solution)/shard_map/all_to_all | solution.py:100
  84.1 39.0 %collective-permute-start.2 = (bf16[1,1024,128]{2,1,0:T(8,128)(2,1)S(1)}, bf16[1,1024,128]{2,1,0:T(8,128)(2,1)S(1)}, u32[]{:S(2)}, u32[]{:S(2)}) collective-permute-start(bf16[1,1024,128]{2,1,0:T(8,128)(2,1)S(1)} %broadcast_select_fusion), channel_id=1, source_target_pairs={{0,64},{1,193},{2,66},{3,195},{4,68},{5,197},{6,70},{7,199},{64,12... | collective-permute-start | bytes 786440 | tf_op jit(solution)/shard_map/ppermute | solution.py:35
  124.3 13.9 %all-to-all-start.2 = ((bf16[4,1,1024,128]{3,2,1,0:T(8,128)(2,1)}), bf16[4,1,1024,128]{3,2,1,0:T(8,128)(2,1)S(1)}, u32[]{:S(2)}, u32[]{:S(2)}) async-start(bf16[4,1,1024,128]{3,2,1,0:T(8,128)(2,1)} %broadcast_in_dim.19), calls=%async_computation.2 | async-start | bytes 2097152 | tf_op jit(solution)/shard_map/all_to_all | solution.py:100
